TPU v7x, 32 devices: a whole 2x2x4 slice. The times are simulated.
32 devices in a mesh: section: 4 (over z), seq: 8 (over y, x, core).
Axes of the slice: x: 2, y: 2, z: 4, core: 2. Of those that a mesh axis runs over, the one named last changes fastest.
Arguments:
- queries: bfloat16 [4, 1024, 8192], P('section', 'seq'), may hold values from -24 to 24
- keys: bfloat16 [4, 1024, 1024], P('section', 'seq'), may hold values from -24 to 24
- values: bfloat16 [4, 1024, 1024], P('section', 'seq'), may hold values from -6 to 6
- block_mask: int32 [4, 8, 8], P('section'), may hold values from 0 to 1, as said below
- block_live: int32 [4, 8], P('section'), may hold values from 1 to 128, as said below
Outputs:
- passed_context: bfloat16 [4, 1024, 8192], P('section', 'seq')
Inputs may be any that keep to these rules, and one draw needn't show every extreme that they name: block_mask[m, i, j] is 1 exactly when block j is block i or one of its ancestors in micro-batch m's tree: the first 4 blocks form a chain, each later block hangs below the chain's last block or a later block of lower index. `block_live`: the first 4 blocks of every micro-batch are full, its last block holds one live token.
All inputs are finite; a program needn't handle non-finite values.
Results may differ from a plain program's by a relative error of at most 0.0049.
Values may be sent and summed in bfloat16 or wider, within the bound.
No kernel may reach another device: no remote copies, remote signals or barrier semaphores. Data moves between devices by JAX's collectives and lax.ppermute only.
A program may use at most 128 MiB of HBM per device.

v0:
```python
import functools

import jax
import jax.numpy as jnp
from jax import lax
from jax.experimental import pallas as pl
from jax.experimental.pallas import tpu as pltpu
from jax.sharding import PartitionSpec as P

HEAD_SIZE = 128
NEG = -1e30
COST = pl.CostEstimate(flops=1, bytes_accessed=1, transcendentals=0)


def attend_kernel(scale, mask, live, q_ref, kv_ref, o_ref, bias, scores, peak, total):
    rows = q_ref.shape[0]
    group = q_ref.shape[1] // HEAD_SIZE
    blocks = [kv_ref.at[j] for j in range(kv_ref.shape[0])]
    width = blocks[0].shape[0]
    span = 2 * width
    me = lax.axis_index("seq")
    allowed = [mask[me, b] for b in range(len(blocks))]
    pairs = range(len(blocks) // 2)
    needed = [allowed[2 * t] + allowed[2 * t + 1] > 0 for t in pairs]

    @pl.when(pl.program_id(0) == 0)
    def _():
        row = lax.broadcasted_iota(jnp.int32, (rows, width), 0)
        col = lax.broadcasted_iota(jnp.int32, (rows, width), 1)
        for p in range(len(blocks)):
            limit = jnp.where(allowed[p] == 1, live[p], 0)
            reach = jnp.where(p == me, row, rows)
            bias[:, p * width : (p + 1) * width] = jnp.where(
                (col < limit) & (col <= reach), 0.0, NEG
            )

    peak[...] = jnp.full_like(peak, NEG)
    total[...] = jnp.zeros_like(total)
    for t in pairs:

        @pl.when(needed[t])
        def _():
            q = jnp.concatenate(
                [q_ref[:, g * HEAD_SIZE : (g + 1) * HEAD_SIZE] for g in range(group)], axis=0
            )
            keys = jnp.concatenate(
                [blocks[2 * t][:, :HEAD_SIZE], blocks[2 * t + 1][:, :HEAD_SIZE]], axis=0
            )
            part = lax.dot_general(
                q, keys, (((1,), (1,)), ((), ())), preferred_element_type=jnp.float32
            )
            part = part.reshape(group, rows, span) + bias[:, t * span : (t + 1) * span][None]
            part = part.reshape(group * rows, span)
            scores[:, t * span : (t + 1) * span] = part
            here = jnp.maximum(part[:, :width], part[:, width:])
            peak[...] = jnp.maximum(peak[...], here)

    top = jnp.max(peak[...], axis=1, keepdims=True)
    peak[...] = jnp.broadcast_to(top, peak.shape)
    for t in pairs:

        @pl.when(needed[t])
        def _():
            highest = jnp.concatenate([peak[...], peak[...]], axis=1)
            expo = jnp.exp2((scores[:, t * span : (t + 1) * span] - highest) * scale)
            vals = jnp.concatenate(
                [blocks[2 * t][:, HEAD_SIZE:], blocks[2 * t + 1][:, HEAD_SIZE:]], axis=0
            )
            both = jnp.concatenate([vals, jnp.ones((span, HEAD_SIZE), jnp.bfloat16)], axis=1)
            total[...] += jnp.dot(
                expo.astype(jnp.bfloat16), both, preferred_element_type=jnp.float32
            )

    alive = lax.broadcasted_iota(jnp.int32, (rows, HEAD_SIZE), 0) < live[me]
    for g in range(group):
        one = total[g * rows : (g + 1) * rows]
        out = jnp.where(alive, one[:, :HEAD_SIZE] / one[:, HEAD_SIZE:], 0.0)
        o_ref[:, g * HEAD_SIZE : (g + 1) * HEAD_SIZE] = out.astype(jnp.bfloat16)


def attend(mask, live, queries, first, heads, group, kv):
    rows = queries.shape[0]
    count, width = kv.shape[:2]
    step = group * HEAD_SIZE
    scale = HEAD_SIZE**-0.5 * 1.4426950408889634
    smem = pl.BlockSpec(memory_space=pltpu.SMEM)
    return pl.pallas_call(
        functools.partial(attend_kernel, scale),
        grid=(heads,),
        out_shape=jax.ShapeDtypeStruct((rows, heads * step), jnp.bfloat16),
        in_specs=[
            smem,
            smem,
            pl.BlockSpec((rows, step), lambda h: (0, first + h)),
            pl.BlockSpec((count, width, 2 * HEAD_SIZE), lambda h: (0, 0, h)),
        ],
        out_specs=pl.BlockSpec((rows, step), lambda h: (0, h)),
        scratch_shapes=[
            pltpu.VMEM((rows, count * width), jnp.float32),
            pltpu.VMEM((group * rows, count * width), jnp.float32),
            pltpu.VMEM((group * rows, width), jnp.float32),
            pltpu.VMEM((group * rows, 2 * HEAD_SIZE), jnp.float32),
        ],
        compiler_params=pltpu.CompilerParams(vmem_limit_bytes=40 * 2**20),
        cost_estimate=COST,
    )(mask, live, queries, kv)


def planar_kernel(scale, mask, live, q_ref, mine, theirs, o_ref):
    rows = q_ref.shape[0]
    group = q_ref.shape[1] // HEAD_SIZE
    chips, width = mine.shape[:2]
    me = lax.axis_index("seq")
    chip, core = me // 2, me % 2

    def body(n):
        slot = lax.broadcasted_iota(jnp.int32, (width, HEAD_SIZE), 0)
        zeroth = jnp.where(
            core == 0,
            mine[n - 1, :1, :HEAD_SIZE].astype(jnp.float32),
            theirs[n - 1, :1, :HEAD_SIZE].astype(jnp.float32),
        )
        zeroth = jnp.broadcast_to(zeroth, (width, HEAD_SIZE)).astype(jnp.bfloat16)
        keys, vals = [], []
        for j in range(n):
            r = (n - 1) ^ j
            for ref, block in ((mine, 2 * j + core), (theirs, 2 * j + 1 - core)):
                there = slot < jnp.where(mask[me, block] == 1, live[block], 0)
                if r == 0 and ref is mine:
                    keys.append(ref[r, :, :HEAD_SIZE])
                else:
                    keys.append(jnp.where(there, ref[r, :, :HEAD_SIZE], zeroth))
                vals.append(
                    jnp.concatenate(
                        [
                            jnp.where(there, ref[r, :, HEAD_SIZE:], jnp.bfloat16(0)),
                            jnp.where(there, jnp.bfloat16(1), jnp.bfloat16(0)),
                        ],
                        axis=1,
                    )
                )
        pairs = [jnp.concatenate(keys[2 * j : 2 * j + 2], axis=0) for j in range(n)]
        vals = jnp.concatenate(vals, axis=0)
        row = lax.broadcasted_iota(jnp.int32, (rows, width), 0)
        col = lax.broadcasted_iota(jnp.int32, (rows, width), 1)
        bias = jnp.where((col < live[me]) & (col <= row), 0.0, NEG)
        alive = lax.broadcasted_iota(jnp.int32, (rows, HEAD_SIZE), 0) < live[me]
        for g in range(group):
            cols = slice(g * HEAD_SIZE, (g + 1) * HEAD_SIZE)
            q = q_ref[:, cols]
            scores = []
            for j in range(n):
                part = lax.dot_general(
                    q, pairs[j], (((1,), (1,)), ((), ())), preferred_element_type=jnp.float32
                )
                own, other = part[:, :width], part[:, width:]
                scores += [own + bias if j == n - 1 else own, other]
            top = functools.reduce(jnp.maximum, scores)
            top = jnp.max(top, axis=1, keepdims=True)
            expo = [jnp.exp2((one - top) * scale).astype(jnp.bfloat16) for one in scores]
            out = jnp.dot(jnp.concatenate(expo, axis=1), vals, preferred_element_type=jnp.float32)
            out = jnp.where(alive, out[:, :HEAD_SIZE] / out[:, HEAD_SIZE:], 0.0)
            o_ref[:, cols] = out.astype(jnp.bfloat16)

    for n in range(1, chips + 1):
        pl.when(chip == n - 1)(functools.partial(body, n))


def attend_planar(mask, live, queries, first, group, mine, theirs, heads):
    rows = queries.shape[0]
    step = group * HEAD_SIZE
    smem = pl.BlockSpec(memory_space=pltpu.SMEM)
    kv = pl.BlockSpec(mine.shape[:2] + (2 * HEAD_SIZE,), lambda i: (0, 0, i))
    return pl.pallas_call(
        functools.partial(planar_kernel, HEAD_SIZE**-0.5 * 1.4426950408889634),
        grid=(heads,),
        out_shape=jax.ShapeDtypeStruct((rows, heads * step), jnp.bfloat16),
        in_specs=[smem, smem, pl.BlockSpec((rows, step), lambda i: (0, first + i)), kv, kv],
        out_specs=pl.BlockSpec((rows, step), lambda i: (0, i)),
        compiler_params=pltpu.CompilerParams(vmem_limit_bytes=40 * 2**20),
        cost_estimate=COST,
    )(mask, live, queries, mine, theirs)


def pack_heads(k_ref, v_ref, first, ref, count):
    for i in range(count):
        cols = slice((first + i) * HEAD_SIZE, (first + i + 1) * HEAD_SIZE)
        ref[:, 2 * i * HEAD_SIZE : (2 * i + 1) * HEAD_SIZE] = k_ref[:, cols]
        ref[:, (2 * i + 1) * HEAD_SIZE : (2 * i + 2) * HEAD_SIZE] = v_ref[:, cols]


def ahead_kernel(k_ref, v_ref, sent):
    pack_heads(k_ref, v_ref, 0, sent, sent.shape[1] // (2 * HEAD_SIZE))


def pack_ahead(keys, values, heads):
    rows = keys.shape[0]
    shape = (rows, heads * 2 * HEAD_SIZE)
    kv = whole((rows, heads * HEAD_SIZE))
    return pl.pallas_call(
        ahead_kernel,
        grid=(1,),
        out_shape=jax.ShapeDtypeStruct(shape, keys.dtype),
        in_specs=[kv, kv],
        out_specs=whole(shape),
        cost_estimate=COST,
    )(keys, values)


def rest_kernel(first, mask, live, q_ref, k_ref, v_ref, sent, q_sent, part):
    pack_heads(k_ref, v_ref, first, part, part.shape[1] // (2 * HEAD_SIZE))
    last = q_ref.shape[1]
    q_sent[:, :last] = q_ref[...]
    q_sent[:, last:] = jnp.zeros_like(q_sent[:, last:])
    blocks = live.shape[0]
    deep = 16
    row = lax.broadcasted_iota(jnp.int32, (deep, HEAD_SIZE), 0)
    col = lax.broadcasted_iota(jnp.int32, (deep, HEAD_SIZE), 1)
    tile = jnp.zeros((deep, HEAD_SIZE), jnp.int32)
    for j in range(blocks):
        tile = jnp.where((row == blocks) & (col == j), live[j], tile)
        for i in range(blocks):
            tile = jnp.where((row == i) & (col == j), mask[i, j], tile)
    q_sent[:deep, last:] = tile.astype(jnp.float32).astype(q_sent.dtype)


def whole(shape):
    return pl.BlockSpec(shape, lambda i: (0, 0))


def pack_rest(mask, live, queries, keys, values, first, sent):
    rows, cols = keys.shape
    q_cols = queries.shape[1] // (cols // HEAD_SIZE) * first
    smem = pl.BlockSpec(memory_space=pltpu.SMEM)
    shapes = [(rows, q_cols + HEAD_SIZE), (rows, 2 * (cols - first * HEAD_SIZE))]
    return pl.pallas_call(
        functools.partial(rest_kernel, first),
        grid=(1,),
        out_shape=[jax.ShapeDtypeStruct(shape, keys.dtype) for shape in shapes],
        in_specs=[smem, smem, whole((rows, q_cols)), whole(keys.shape), whole(values.shape)]
        + [pl.BlockSpec(memory_space=pl.ANY)],
        out_specs=[whole(shape) for shape in shapes],
        cost_estimate=COST,
    )(mask, live, queries, keys, values, sent)


def pack_pairs(keys, values, heads):
    parts = []
    for h in heads:
        cols = slice(h * HEAD_SIZE, (h + 1) * HEAD_SIZE)
        parts += [keys[:, cols], values[:, cols]]
    return jnp.concatenate(parts, axis=1)


def after(value, *others):
    return lax.optimization_barrier((value,) + others)[0] if others else value


def on_plane(nsec, to):
    return [(s * 8 + i, s * 8 + to(i)) for s in range(nsec) for i in range(8)]


def exchange(part, nsec, by):
    return lax.ppermute(part, ("section", "seq"), on_plane(nsec, lambda i: i ^ by))


def per_device_8(queries, keys, values, block_mask, block_live):
    nsec = lax.axis_size("section")
    kv_heads = keys.shape[2] // HEAD_SIZE
    group = queries.shape[2] // keys.shape[2]
    step = group * HEAD_SIZE
    q, k, v = queries[0], keys[0], values[0]
    mask, live = block_mask[0], block_live[0]
    onward = [(i, (i + 1) % nsec) for i in range(nsec)]
    half = kv_heads // 2

    def on(value):
        return lax.ppermute(value, "section", onward)

    def gather(part, count, *before):
        pieces = [part] + [exchange(part, nsec, by) for by in (2, 4)]
        pieces.append(exchange(after(part, *before), nsec, 6))
        width = part.shape[1] // count
        return [jnp.stack([p[:, i * width : (i + 1) * width] for p in pieces]) for i in range(count)]

    def both_cores(mines):
        return mines, [exchange(mine, nsec, 1) for mine in mines]

    def joined(arrays):
        return jnp.concatenate(arrays, axis=2) if len(arrays) > 1 else arrays[0]

    sent = pack_ahead(k, v, half)
    q_sent, part1 = pack_rest(mask, live, q, k, v, half, sent)
    sent_in, q_in = on(sent), on(q_sent)

    mines1 = gather(part1, 4, sent_in)
    kvs1 = [joined(arrays) for arrays in both_cores(mines1)]
    ctx = attend_planar(mask, live, q, half, group, *kvs1, half)
    out = on(ctx)

    part0 = after(sent_in, *mines1)
    mines0 = gather(part0, 2, ctx, q_in)
    mines0 = lax.optimization_barrier((*mines0, ctx))[:2]
    mines0, theirs0 = both_cores(mines0)
    blocks = live.shape[0]
    tab = q_in[: blocks + 1, half * step :][:, :blocks].astype(jnp.int32)
    mask_in, live_in = tab[:-1], tab[-1]
    heads = half // 2
    first = [
        attend_planar(mask_in, live_in, q_in, i * heads, group, mines0[i], theirs0[i], heads)
        for i in range(2)
    ]
    return jnp.concatenate(first + [out], axis=1)[None]


def per_device(queries, keys, values, block_mask, block_live):
    nsec = lax.axis_size("section")
    group = queries.shape[2] // keys.shape[2]
    onward = [(i, (i + 1) % nsec) for i in range(nsec)]
    outs = []
    for h in range(0, keys.shape[2] // HEAD_SIZE, 2):
        kv = lax.all_gather(pack_pairs(keys[0], values[0], [h, h + 1]), "seq", axis=0)
        out = attend(block_mask[0], block_live[0], queries[0], h, 2, group, kv)
        outs.append(lax.ppermute(out, "section", onward))
    return jnp.concatenate(outs, axis=1)[None]


def solution(mesh):
    placed = (
        P("section", "seq", None),
        P("section", "seq", None),
        P("section", "seq", None),
        P("section", None, None),
        P("section", None),
    )
    body = per_device_8 if mesh.shape["seq"] == 8 else per_device
    return jax.shard_map(
        body, mesh=mesh, in_specs=placed, out_specs=P("section", "seq", None), check_vma=False
    )
```

profile of v0, /device:TPU:0, one launch (start us, length us, event | category | flops | bytes accessed | tf_op | source)
XLA Modules:
  0.0 61.0 jit_solution(3319160349792436381)
XLA Ops:
  0.0 1.7 %shard_map.55.sent = bf16[128,1024]{1,0:T(8,128)(2,1)} custom-call(bf16[128,1024]{1,0:T(8,128)(2,1)} %bitcast.63, bf16[128,1024]{1,0:T(8,128)(2,1)} %bitcast.65), custom_call_target="tpu_custom_call" | custom-call | flops 1 | bytes 1 | tf_op jit(solution)/shard_map/pallas_call | solution.py:200
  1.7 3.0 %collective-permute-start.1 = (bf16[128,1024]{1,0:T(8,128)(2,1)}, bf16[128,1024]{1,0:T(8,128)(2,1)S(1)}, u32[]{:S(2)}, u32[]{:S(2)}) collective-permute-start(bf16[128,1024]{1,0:T(8,128)(2,1)} %shard_map.55.sent), channel_id=1, source_target_pairs={{0,8},{8,16},{16,24},{24,0},{1,9},{9,17},{17,25},{25,1},{2,10},{10... | collective-permute-start | bytes 786440 | tf_op jit(solution)/shard_map/ppermute | solution.py:278
  4.8 2.5 %shard_map.56 = (bf16[128,4224]{1,0:T(8,128)(2,1)}, bf16[128,1024]{1,0:T(8,128)(2,1)}) custom-call(s32[8,8]{1,0:T(8,128)} %bitcast.59, s32[8]{0:T(128)} %bitcast.61, bf16[128,8192]{1,0:T(8,128)(2,1)} %bitcast.57, bf16[128,1024]{1,0:T(8,128)(2,1)} %bitcast.64, bf16[128,1024]{1,0:T(8,128)(2,1)} %bitcast.66, bf16[128,1024]{1,0:T(8,128)(2,1)} %shard_map.55.sent), custom_call_target="tpu_custom_call" | custom-call | flops 1 | bytes 1 | tf_op jit(solution)/shard_map/pallas_call | solution.py:236
  7.3 1.5 %collective-permute-start.2 = (bf16[128,1024]{1,0:T(8,128)(2,1)}, bf16[128,1024]{1,0:T(8,128)(2,1)S(1)}, u32[]{:S(2)}, u32[]{:S(2)}) collective-permute-start(bf16[128,1024]{1,0:T(8,128)(2,1)} %get-tuple-element.14), channel_id=1, source_target_pairs={{0,2},{1,3},{2,0},{3,1},{4,6},{5,7},{6,4},{7,5},{8,10},{9,11},{10,... | collective-permute-start | bytes 786440 | tf_op jit(solution)/shard_map/ppermute | solution.py:264
  8.7 1.5 %collective-permute-start.3 = (bf16[128,1024]{1,0:T(8,128)(2,1)}, bf16[128,1024]{1,0:T(8,128)(2,1)S(1)}, u32[]{:S(2)}, u32[]{:S(2)}) collective-permute-start(bf16[128,1024]{1,0:T(8,128)(2,1)} %get-tuple-element.14), channel_id=1, source_target_pairs={{0,4},{1,5},{2,6},{3,7},{4,0},{5,1},{6,2},{7,3},{8,12},{9,13},{10,... | collective-permute-start | bytes 786440 | tf_op jit(solution)/shard_map/ppermute | solution.py:264
  10.3 1.6 %collective-permute-start = (bf16[128,4224]{1,0:T(8,128)(2,1)}, bf16[128,4224]{1,0:T(8,128)(2,1)S(1)}, u32[]{:S(2)}, u32[]{:S(2)}) collective-permute-start(bf16[128,4224]{1,0:T(8,128)(2,1)} %get-tuple-element.12), channel_id=1, source_target_pairs={{0,8},{8,16},{16,24},{24,0},{1,9},{9,17},{17,25},{25,1},{2,10},{10... | collective-permute-start | bytes 3244040 | tf_op jit(solution)/shard_map/ppermute | solution.py:278
  11.8 1.0 %slice_bitcast_fusion.23 = (bf16[1,128,256]{2,1,0:T(8,128)(2,1)S(1)}, bf16[1,128,256]{2,1,0:T(8,128)(2,1)S(1)}, bf16[1,128,256]{2,1,0:T(8,128)(2,1)S(1)}, bf16[1,128,256]{2,1,0:T(8,128)(2,1)S(1)}) fusion(bf16[128,1024]{1,0:T(8,128)(2,1)} %get-tuple-element.14), kind=kLoop, calls=%fused_computation.32 | loop fusion | bytes 524288 | tf_op jit(solution)/shard_map/stack | solution.py:284
  12.8 0.5 collective-permute-done.1
  13.3 3.5 %collective-permute-start.4 = (bf16[128,1024]{1,0:T(8,128)(2,1)}, bf16[128,1024]{1,0:T(8,128)(2,1)S(1)}, u32[]{:S(2)}, u32[]{:S(2)}) collective-permute-start(bf16[128,1024]{1,0:T(8,128)(2,1)} %get-tuple-element.14), channel_id=1, source_target_pairs={{0,6},{1,7},{2,4},{3,5},{4,2},{5,3},{6,0},{7,1},{8,14},{9,15},{10,... | collective-permute-start | bytes 786440 | tf_op jit(solution)/shard_map/ppermute | solution.py:264
  16.8 5.2 %collective-permute-done.3 = bf16[128,1024]{1,0:T(8,128)(2,1)S(1)} collective-permute-done((bf16[128,1024]{1,0:T(8,128)(2,1)}, bf16[128,1024]{1,0:T(8,128)(2,1)S(1)}, u32[]{:S(2)}, u32[]{:S(2)}) %collective-permute-start.3) | collective-permute-done | bytes 262176 | tf_op jit(solution)/shard_map/ppermute | solution.py:264
  22.2 0.1 collective-permute-start.7
  22.3 0.6 collective-permute-start.8
  22.9 0.1 collective-permute-start.9
  23.0 0.0 copy-start
  23.0 0.6 collective-permute-start.10
  23.6 0.1 maximum_maximum_fusion.mine
  23.7 0.0 collective-permute-done.7
  23.8 1.3 %collective-permute-start.5 = (bf16[128,1024]{1,0:T(8,128)(2,1)S(1)}, bf16[128,1024]{1,0:T(8,128)(2,1)S(1)}, u32[]{:S(2)}, u32[]{:S(2)}) collective-permute-start(bf16[128,1024]{1,0:T(8,128)(2,1)S(1)} %collective-permute-done.1), channel_id=1, source_target_pairs={{0,2},{1,3},{2,0},{3,1},{4,6},{5,7},{6,4},{7,5},{8,10},{9,11},{10,... | collective-permute-start | bytes 786440 | tf_op jit(solution)/shard_map/ppermute | solution.py:264
  25.0 1.6 %collective-permute-start.6 = (bf16[128,1024]{1,0:T(8,128)(2,1)S(1)}, bf16[128,1024]{1,0:T(8,128)(2,1)S(1)}, u32[]{:S(2)}, u32[]{:S(2)}) collective-permute-start(bf16[128,1024]{1,0:T(8,128)(2,1)S(1)} %collective-permute-done.1), channel_id=1, source_target_pairs={{0,4},{1,5},{2,6},{3,7},{4,0},{5,1},{6,2},{7,3},{8,12},{9,13},{10,... | collective-permute-start | bytes 786440 | tf_op jit(solution)/shard_map/ppermute | solution.py:264
  26.6 0.1 pad_maximum_fusion.theirs
  26.8 3.8 %shard_map.57 = bf16[128,4096]{1,0:T(8,128)(2,1)S(1)} custom-call(s32[8,8]{1,0:T(8,128)S(1)} %bitcast.60, s32[8]{0:T(128)S(1)} %bitcast.62, bf16[128,8192]{1,0:T(8,128)(2,1)S(1)} %bitcast.58, bf16[4,128,1024]{2,1,0:T(8,128)(2,1)S(1)} %maximum_maximum_fusion.mine, bf16[4,128,1024]{2,1,0:T(8,128)(2,1)S(1)} %pad_maximum_fusion.theirs), custom_call_target="tpu_custom_call" | custom-call | flops 1 | bytes 1 | tf_op jit(solution)/shard_map/pallas_call | solution.py:174
  30.6 1.1 %collective-permute-start.14 = (bf16[128,4096]{1,0:T(8,128)(2,1)S(1)}, bf16[128,4096]{1,0:T(8,128)(2,1)S(1)}, u32[]{:S(2)}, u32[]{:S(2)}) collective-permute-start(bf16[128,4096]{1,0:T(8,128)(2,1)S(1)} %shard_map.57), channel_id=1, source_target_pairs={{0,8},{8,16},{16,24},{24,0},{1,9},{9,17},{17,25},{25,1},{2,10},{10... | collective-permute-start | bytes 3145736 | tf_op jit(solution)/shard_map/ppermute | solution.py:278
  31.7 7.4 %collective-permute-done.q_ref = bf16[128,4224]{1,0:T(8,128)(2,1)S(1)} collective-permute-done((bf16[128,4224]{1,0:T(8,128)(2,1)}, bf16[128,4224]{1,0:T(8,128)(2,1)S(1)}, u32[]{:S(2)}, u32[]{:S(2)}) %collective-permute-start) | collective-permute-done | bytes 1081376 | tf_op jit(solution)/shard_map/ppermute | solution.py:278
  39.1 7.2 %collective-permute-done.11 = bf16[128,1024]{1,0:T(8,128)(2,1)S(1)} collective-permute-done((bf16[128,1024]{1,0:T(8,128)(2,1)S(1)}, bf16[128,1024]{1,0:T(8,128)(2,1)S(1)}, u32[]{:S(2)}, u32[]{:S(2)}) %collective-permute-start.11) | collective-permute-done | bytes 262176 | tf_op jit(solution)/shard_map/ppermute | solution.py:264
  46.4 0.1 pad_maximum_fusion.1
  46.5 0.1 collective-permute-start.12
  46.6 0.5 collective-permute-start.13
  47.1 1.4 %collective-permute-done.12.theirs = bf16[4,128,512]{2,1,0:T(8,128)(2,1)S(1)} collective-permute-done((bf16[4,128,512]{2,1,0:T(8,128)(2,1)S(1)}, bf16[4,128,512]{2,1,0:T(8,128)(2,1)S(1)}, u32[]{:S(2)}, u32[]{:S(2)}) %collective-permute-start.12) | collective-permute-done | bytes 524320 | tf_op jit(solution)/shard_map/ppermute | solution.py:264
  48.5 2.1 %shard_map.58 = bf16[128,2048]{1,0:T(8,128)(2,1)S(1)} custom-call(s32[8,8]{1,0:T(8,128)S(1)} %slice.111.mask, s32[8]{0:T(128)S(1)} %slice_bitcast_fusion.24.live, bf16[128,4224]{1,0:T(8,128)(2,1)S(1)} %collective-permute-done.q_ref, bf16[4,128,512]{2,1,0:T(8,128)(2,1)S(1)} %get-tuple-element.17.mine, bf16[4,128,512]{2,1,0:T(8,128)(2,1)S(1)} %collective-permute-done.12.theirs), custom_call_target="tpu_custom_call" | custom-call | flops 1 | bytes 1 | tf_op jit(solution)/shard_map/pallas_call | solution.py:174
  50.6 2.2 %shard_map.59 = bf16[128,2048]{1,0:T(8,128)(2,1)S(1)} custom-call(s32[8,8]{1,0:T(8,128)S(1)} %slice.111.mask, s32[8]{0:T(128)S(1)} %slice_bitcast_fusion.24.live, bf16[128,4224]{1,0:T(8,128)(2,1)S(1)} %collective-permute-done.q_ref, bf16[4,128,512]{2,1,0:T(8,128)(2,1)S(1)} %get-tuple-element.18.mine, bf16[4,128,512]{2,1,0:T(8,128)(2,1)S(1)} %collective-permute-done.13.theirs), custom_call_target="tpu_custom_call" | custom-call | flops 1 | bytes 1 | tf_op jit(solution)/shard_map/pallas_call | solution.py:174
  52.8 6.7 %collective-permute-done.14 = bf16[128,4096]{1,0:T(8,128)(2,1)S(1)} collective-permute-done((bf16[128,4096]{1,0:T(8,128)(2,1)S(1)}, bf16[128,4096]{1,0:T(8,128)(2,1)S(1)}, u32[]{:S(2)}, u32[]{:S(2)}) %collective-permute-start.14) | collective-permute-done | bytes 1048608 | tf_op jit(solution)/shard_map/ppermute | solution.py:278
  59.5 1.5 %maximum_bitcast_fusion = bf16[1,128,8192]{2,1,0:T(8,128)(2,1)} fusion(bf16[128,4096]{1,0:T(8,128)(2,1)S(1)} %collective-permute-done.14, bf16[128,2048]{1,0:T(8,128)(2,1)S(1)} %shard_map.59, bf16[128,2048]{1,0:T(8,128)(2,1)S(1)} %shard_map.58), kind=kLoop, calls=%fused_computation | loop fusion | flops 6291456 | bytes 4194304 | tf_op jit(solution)/shard_map/broadcast_in_dim | solution.py:313
  (28 shorter events, 0.3 us)
Async XLA Ops:
  1.7 11.6 %collective-permute-start.1 = (bf16[128,1024]{1,0:T(8,128)(2,1)}, bf16[128,1024]{1,0:T(8,128)(2,1)S(1)}, u32[]{:S(2)}, u32[]{:S(2)}) collective-permute-start(bf16[128,1024]{1,0:T(8,128)(2,1)} %shard_map.55.sent), channel_id=1, source_target_pairs={{0,8},{8,16},{16,24},{24,0},{1,9},{9,17},{17,25},{25,1},{2,10},{10... | collective-permute-start | bytes 786440 | tf_op jit(solution)/shard_map/ppermute | solution.py:278
  7.3 9.6 %collective-permute-start.2 = (bf16[128,1024]{1,0:T(8,128)(2,1)}, bf16[128,1024]{1,0:T(8,128)(2,1)S(1)}, u32[]{:S(2)}, u32[]{:S(2)}) collective-permute-start(bf16[128,1024]{1,0:T(8,128)(2,1)} %get-tuple-element.14), channel_id=1, source_target_pairs={{0,2},{1,3},{2,0},{3,1},{4,6},{5,7},{6,4},{7,5},{8,10},{9,11},{10,... | collective-permute-start | bytes 786440 | tf_op jit(solution)/shard_map/ppermute | solution.py:264
  8.7 13.3 %collective-permute-start.3 = (bf16[128,1024]{1,0:T(8,128)(2,1)}, bf16[128,1024]{1,0:T(8,128)(2,1)S(1)}, u32[]{:S(2)}, u32[]{:S(2)}) collective-permute-start(bf16[128,1024]{1,0:T(8,128)(2,1)} %get-tuple-element.14), channel_id=1, source_target_pairs={{0,4},{1,5},{2,6},{3,7},{4,0},{5,1},{6,2},{7,3},{8,12},{9,13},{10,... | collective-permute-start | bytes 786440 | tf_op jit(solution)/shard_map/ppermute | solution.py:264
  10.3 28.8 %collective-permute-start = (bf16[128,4224]{1,0:T(8,128)(2,1)}, bf16[128,4224]{1,0:T(8,128)(2,1)S(1)}, u32[]{:S(2)}, u32[]{:S(2)}) collective-permute-start(bf16[128,4224]{1,0:T(8,128)(2,1)} %get-tuple-element.12), channel_id=1, source_target_pairs={{0,8},{8,16},{16,24},{24,0},{1,9},{9,17},{17,25},{25,1},{2,10},{10... | collective-permute-start | bytes 3244040 | tf_op jit(solution)/shard_map/ppermute | solution.py:278
  13.3 8.8 %collective-permute-start.4 = (bf16[128,1024]{1,0:T(8,128)(2,1)}, bf16[128,1024]{1,0:T(8,128)(2,1)S(1)}, u32[]{:S(2)}, u32[]{:S(2)}) collective-permute-start(bf16[128,1024]{1,0:T(8,128)(2,1)} %get-tuple-element.14), channel_id=1, source_target_pairs={{0,6},{1,7},{2,4},{3,5},{4,2},{5,3},{6,0},{7,1},{8,14},{9,15},{10,... | collective-permute-start | bytes 786440 | tf_op jit(solution)/shard_map/ppermute | solution.py:264
  22.2 1.6 %collective-permute-start.7 = (bf16[4,128,256]{2,1,0:T(8,128)(2,1)S(1)}, bf16[4,128,256]{2,1,0:T(8,128)(2,1)S(1)}, u32[]{:S(2)}, u32[]{:S(2)}) collective-permute-start(bf16[4,128,256]{2,1,0:T(8,128)(2,1)S(1)} %pad_maximum_fusion.3), channel_id=1, source_target_pairs={{0,1},{1,0},{2,3},{3,2},{4,5},{5,4},{6,7},{7,6},{8,9},{9,8},{10,11... | collective-permute-start | bytes 786440 | tf_op jit(solution)/shard_map/ppermute | solution.py:264
  22.3 2.7 %collective-permute-start.8 = (bf16[4,128,256]{2,1,0:T(8,128)(2,1)S(1)}, bf16[4,128,256]{2,1,0:T(8,128)(2,1)S(1)}, u32[]{:S(2)}, u32[]{:S(2)}) collective-permute-start(bf16[4,128,256]{2,1,0:T(8,128)(2,1)S(1)} %pad_maximum_fusion.4), channel_id=1, source_target_pairs={{0,1},{1,0},{2,3},{3,2},{4,5},{5,4},{6,7},{7,6},{8,9},{9,8},{10,11... | collective-permute-start | bytes 786440 | tf_op jit(solution)/shard_map/ppermute | solution.py:264
  22.9 3.7 %collective-permute-start.9 = (bf16[4,128,256]{2,1,0:T(8,128)(2,1)S(1)}, bf16[4,128,256]{2,1,0:T(8,128)(2,1)S(1)}, u32[]{:S(2)}, u32[]{:S(2)}) collective-permute-start(bf16[4,128,256]{2,1,0:T(8,128)(2,1)S(1)} %pad_maximum_fusion.5), channel_id=1, source_target_pairs={{0,1},{1,0},{2,3},{3,2},{4,5},{5,4},{6,7},{7,6},{8,9},{9,8},{10,11... | collective-permute-start | bytes 786440 | tf_op jit(solution)/shard_map/ppermute | solution.py:264
  23.0 3.8 %copy-start = (bf16[1,128,8192]{2,1,0:T(8,128)(2,1)S(1)}, bf16[1,128,8192]{2,1,0:T(8,128)(2,1)}, u32[]{:S(2)}) copy-start(bf16[1,128,8192]{2,1,0:T(8,128)(2,1)} %param.5) | copy-start | bytes 6291460
  23.0 3.8 %copy-start.1 = (s32[1,8,8]{2,1,0:T(8,128)S(1)}, s32[1,8,8]{2,1,0:T(8,128)}, u32[]{:S(2)}) copy-start(s32[1,8,8]{2,1,0:T(8,128)} %param.8) | copy-start | bytes 772
  23.0 3.8 %copy-start.2 = (s32[1,8]{1,0:T(1,128)S(1)}, s32[1,8]{1,0:T(1,128)}, u32[]{:S(2)}) copy-start(s32[1,8]{1,0:T(1,128)} %param.9) | copy-start | bytes 100
  23.0 3.6 %collective-permute-start.10 = (bf16[4,128,256]{2,1,0:T(8,128)(2,1)S(1)}, bf16[4,128,256]{2,1,0:T(8,128)(2,1)S(1)}, u32[]{:S(2)}, u32[]{:S(2)}) collective-permute-start(bf16[4,128,256]{2,1,0:T(8,128)(2,1)S(1)} %pad_maximum_fusion.6), channel_id=1, source_target_pairs={{0,1},{1,0},{2,3},{3,2},{4,5},{5,4},{6,7},{7,6},{8,9},{9,8},{10,11... | collective-permute-start | bytes 786440 | tf_op jit(solution)/shard_map/ppermute | solution.py:264
  23.8 15.3 %collective-permute-start.5 = (bf16[128,1024]{1,0:T(8,128)(2,1)S(1)}, bf16[128,1024]{1,0:T(8,128)(2,1)S(1)}, u32[]{:S(2)}, u32[]{:S(2)}) collective-permute-start(bf16[128,1024]{1,0:T(8,128)(2,1)S(1)} %collective-permute-done.1), channel_id=1, source_target_pairs={{0,2},{1,3},{2,0},{3,1},{4,6},{5,7},{6,4},{7,5},{8,10},{9,11},{10,... | collective-permute-start | bytes 786440 | tf_op jit(solution)/shard_map/ppermute | solution.py:264
  25.0 14.1 %collective-permute-start.6 = (bf16[128,1024]{1,0:T(8,128)(2,1)S(1)}, bf16[128,1024]{1,0:T(8,128)(2,1)S(1)}, u32[]{:S(2)}, u32[]{:S(2)}) collective-permute-start(bf16[128,1024]{1,0:T(8,128)(2,1)S(1)} %collective-permute-done.1), channel_id=1, source_target_pairs={{0,4},{1,5},{2,6},{3,7},{4,0},{5,1},{6,2},{7,3},{8,12},{9,13},{10,... | collective-permute-start | bytes 786440 | tf_op jit(solution)/shard_map/ppermute | solution.py:264
  30.6 28.9 %collective-permute-start.14 = (bf16[128,4096]{1,0:T(8,128)(2,1)S(1)}, bf16[128,4096]{1,0:T(8,128)(2,1)S(1)}, u32[]{:S(2)}, u32[]{:S(2)}) collective-permute-start(bf16[128,4096]{1,0:T(8,128)(2,1)S(1)} %shard_map.57), channel_id=1, source_target_pairs={{0,8},{8,16},{16,24},{24,0},{1,9},{9,17},{17,25},{25,1},{2,10},{10... | collective-permute-start | bytes 3145736 | tf_op jit(solution)/shard_map/ppermute | solution.py:278
  39.1 7.3 %collective-permute-start.11 = (bf16[128,1024]{1,0:T(8,128)(2,1)S(1)}, bf16[128,1024]{1,0:T(8,128)(2,1)S(1)}, u32[]{:S(2)}, u32[]{:S(2)}) collective-permute-start(bf16[128,1024]{1,0:T(8,128)(2,1)S(1)} %collective-permute-done.1), channel_id=1, source_target_pairs={{0,6},{1,7},{2,4},{3,5},{4,2},{5,3},{6,0},{7,1},{8,14},{9,15},{10,... | collective-permute-start | bytes 786440 | tf_op jit(solution)/shard_map/ppermute | solution.py:264
  46.5 2.0 %collective-permute-start.12 = (bf16[4,128,512]{2,1,0:T(8,128)(2,1)S(1)}, bf16[4,128,512]{2,1,0:T(8,128)(2,1)S(1)}, u32[]{:S(2)}, u32[]{:S(2)}) collective-permute-start(bf16[4,128,512]{2,1,0:T(8,128)(2,1)S(1)} %get-tuple-element.17.mine), channel_id=1, source_target_pairs={{0,1},{1,0},{2,3},{3,2},{4,5},{5,4},{6,7},{7,6},{8,9},{9,8},{10,11... | collective-permute-start | bytes 1572872 | tf_op jit(solution)/shard_map/ppermute | solution.py:264
  46.6 4.0 %collective-permute-start.13 = (bf16[4,128,512]{2,1,0:T(8,128)(2,1)S(1)}, bf16[4,128,512]{2,1,0:T(8,128)(2,1)S(1)}, u32[]{:S(2)}, u32[]{:S(2)}) collective-permute-start(bf16[4,128,512]{2,1,0:T(8,128)(2,1)S(1)} %get-tuple-element.18.mine), channel_id=1, source_target_pairs={{0,1},{1,0},{2,3},{3,2},{4,5},{5,4},{6,7},{7,6},{8,9},{9,8},{10,11... | collective-permute-start | bytes 1572872 | tf_op jit(solution)/shard_map/ppermute | solution.py:264
where the time goes:
time: 61.2 us; the launch traced here: 61 us
  waiting for transfers between devices  28.4 us (46%)
  starting transfers between devices  16.9 us (28%)
  Pallas kernels  12.3 us (20%)
  other arithmetic  2.03 us (3%)
  local copies, waits for them, and re-layouts  1.11 us (2%)
    ppermute x3, waiting for transfers between devices, on(): return lax.ppermute(value, 'section', onward)  14.6 us
    ppermute x12, waiting for transfers between devices, exchange(): lax.ppermute(part, ('section', 'seq'), on_plane(nsec, lambda i: i ^ by))  13.8 us
    ppermute x12, starting transfers between devices, exchange(): lax.ppermute(part, ('section', 'seq'), on_plane(nsec, lambda i: i ^ by))  11.2 us
    pallas_call x3, Pallas kernels, attend_planar(): pl.pallas_call(functools.partial(planar_kernel, HEAD_SIZE ** (-0.5) * 1.4...  8.06 us
    ppermute x3, starting transfers between devices, on(): return lax.ppermute(value, 'section', onward)  5.7 us
    pallas_call x1, Pallas kernels, pack_rest(): pl.pallas_call(functools.partial(rest_kernel, first), grid=(1,), out_shap...  2.5 us
    pallas_call x1, Pallas kernels, pack_ahead(): pl.pallas_call(ahead_kernel, grid=(1,), out_shape=jax.ShapeDtypeStruct(sh...  1.73 us
    broadcast_in_dim x1, other arithmetic, per_device_8(): return jnp.concatenate(first + [out], axis=1)[None]  1.48 us
  transfers between devices with their start and end apart: 15, of which 6 were waited for; matrix products, arithmetic and copies ran while one was open for 3% of the time, Pallas kernels for 17%

commit v1 on v0

--- a/solution.py
+++ b/solution.py
@@ -299,18 +299,15 @@
     out = on(ctx)
 
     part0 = after(sent_in, *mines1)
-    mines0 = gather(part0, 2, ctx, q_in)
-    mines0 = lax.optimization_barrier((*mines0, ctx))[:2]
+    mines0 = gather(part0, 4, ctx, q_in)
+    mines0 = lax.optimization_barrier((*mines0, ctx))[:4]
     mines0, theirs0 = both_cores(mines0)
     blocks = live.shape[0]
     tab = q_in[: blocks + 1, half * step :][:, :blocks].astype(jnp.int32)
     mask_in, live_in = tab[:-1], tab[-1]
-    heads = half // 2
-    first = [
-        attend_planar(mask_in, live_in, q_in, i * heads, group, mines0[i], theirs0[i], heads)
-        for i in range(2)
-    ]
-    return jnp.concatenate(first + [out], axis=1)[None]
+    first = [attend_planar(mask_in, live_in, q_in, 0, group, joined(mines0), joined(theirs0), half)]
+    held = jnp.concatenate(first + [jnp.zeros_like(out)], axis=1)
+    return lax.dynamic_update_slice(lax.optimization_barrier(held), out, (0, half * step))[None]
 
 
 def per_device(queries, keys, values, block_mask, block_live):

time: 61.2 us -> 60.8 us (level)
  waiting for transfers between devices: 28.4 us -> 25.8 us
  local copies, waits for them, and re-layouts: 1.11 us -> 3.66 us
  starting transfers between devices: 16.9 us -> 18.2 us
  other arithmetic: 2.03 us -> 0.81 us
    ppermute x3, waiting for transfers between devices: 14.6 us -> 11.9 us  [on(): return lax.ppermute(value, 'section', onward)]
    concatenate x0 -> x1, local copies, waits for them, and re-layouts: none -> 1.51 us  [per_device_8(): held = jnp.concatenate(first + [jnp.zeros_like(out)], axis=1)]
    broadcast_in_dim x1 -> x0, other arithmetic: 1.48 us -> none  [per_device_8(): return jnp.concatenate(first + [out], axis=1)[None]]
    dynamic_update_slice x0 -> x1, local copies, waits for them, and re-layouts: none -> 1.04 us  [per_device_8(): lax.dynamic_update_slice(lax.optimization_barrier(held), out, (0, half *...]
    ppermute x12 -> x14, starting transfers between devices: 11.2 us -> 12 us  [exchange(): lax.ppermute(part, ('section', 'seq'), on_plane(nsec, lambda i: i ^ by))]
    pallas_call x3 -> x2, Pallas kernels: 8.06 us -> 7.62 us  [attend_planar(): pl.pallas_call(functools.partial(planar_kernel, HEAD_SIZE ** (-0.5) * 1.4...]
    ppermute x12 -> x14, waiting for transfers between devices: 13.8 us -> 13.9 us  [exchange(): lax.ppermute(part, ('section', 'seq'), on_plane(nsec, lambda i: i ^ by))]
  transfers between devices with their start and end apart: 15 -> 17, of which waited for: 6 -> 9; matrix products, arithmetic and copies ran while one was open for 3% -> 6% of each run, Pallas kernels for 17% -> 17%
where the time goes in v1:
time: 60.8 us; the launch traced here: 60.6 us
  waiting for transfers between devices  25.8 us (42%)
  starting transfers between devices  18.2 us (30%)
  Pallas kernels  11.9 us (20%)
  local copies, waits for them, and re-layouts  3.66 us (6%)
  other arithmetic  0.81 us (1%)
    ppermute x14, waiting for transfers between devices, exchange(): lax.ppermute(part, ('section', 'seq'), on_plane(nsec, lambda i: i ^ by))  13.9 us
    ppermute x14, starting transfers between devices, exchange(): lax.ppermute(part, ('section', 'seq'), on_plane(nsec, lambda i: i ^ by))  12 us
    ppermute x3, waiting for transfers between devices, on(): return lax.ppermute(value, 'section', onward)  11.9 us
    pallas_call x2, Pallas kernels, attend_planar(): pl.pallas_call(functools.partial(planar_kernel, HEAD_SIZE ** (-0.5) * 1.4...  7.62 us
    ppermute x3, starting transfers between devices, on(): return lax.ppermute(value, 'section', onward)  6.23 us
    pallas_call x1, Pallas kernels, pack_rest(): pl.pallas_call(functools.partial(rest_kernel, first), grid=(1,), out_shap...  2.5 us
    pallas_call x1, Pallas kernels, pack_ahead(): pl.pallas_call(ahead_kernel, grid=(1,), out_shape=jax.ShapeDtypeStruct(sh...  1.74 us
    concatenate x1, local copies, waits for them, and re-layouts, per_device_8(): held = jnp.concatenate(first + [jnp.zeros_like(out)], axis=1)  1.51 us
  transfers between devices with their start and end apart: 17, of which 9 were waited for; matrix products, arithmetic and copies ran while one was open for 6% of the time, Pallas kernels for 17%

profile of v1, /device:TPU:0, one launch (start us, length us, event | category | flops | bytes accessed | tf_op | source)
XLA Modules:
  0.0 60.6 jit_solution(4556637535276035412)
XLA Ops:
  0.0 1.7 %shard_map.55.sent = bf16[128,1024]{1,0:T(8,128)(2,1)} custom-call(bf16[128,1024]{1,0:T(8,128)(2,1)} %bitcast.81, bf16[128,1024]{1,0:T(8,128)(2,1)} %bitcast.83), custom_call_target="tpu_custom_call" | custom-call | flops 1 | bytes 1 | tf_op jit(solution)/shard_map/pallas_call | solution.py:200
  1.7 3.0 %collective-permute-start.1 = (bf16[128,1024]{1,0:T(8,128)(2,1)}, bf16[128,1024]{1,0:T(8,128)(2,1)S(1)}, u32[]{:S(2)}, u32[]{:S(2)}) collective-permute-start(bf16[128,1024]{1,0:T(8,128)(2,1)} %shard_map.55.sent), channel_id=1, source_target_pairs={{0,8},{8,16},{16,24},{24,0},{1,9},{9,17},{17,25},{25,1},{2,10},{10... | collective-permute-start | bytes 786440 | tf_op jit(solution)/shard_map/ppermute | solution.py:278
  4.8 2.5 %shard_map.56 = (bf16[128,4224]{1,0:T(8,128)(2,1)}, bf16[128,1024]{1,0:T(8,128)(2,1)}) custom-call(s32[8,8]{1,0:T(8,128)} %bitcast.76, s32[8]{0:T(128)} %bitcast.78, bf16[128,8192]{1,0:T(8,128)(2,1)} %bitcast.74, bf16[128,1024]{1,0:T(8,128)(2,1)} %bitcast.82, bf16[128,1024]{1,0:T(8,128)(2,1)} %bitcast.84, bf16[128,1024]{1,0:T(8,128)(2,1)} %shard_map.55.sent), custom_call_target="tpu_custom_call" | custom-call | flops 1 | bytes 1 | tf_op jit(solution)/shard_map/pallas_call | solution.py:236
  7.3 1.5 %collective-permute-start.3 = (bf16[128,1024]{1,0:T(8,128)(2,1)}, bf16[128,1024]{1,0:T(8,128)(2,1)S(1)}, u32[]{:S(2)}, u32[]{:S(2)}) collective-permute-start(bf16[128,1024]{1,0:T(8,128)(2,1)} %get-tuple-element.16), channel_id=1, source_target_pairs={{0,4},{1,5},{2,6},{3,7},{4,0},{5,1},{6,2},{7,3},{8,12},{9,13},{10,... | collective-permute-start | bytes 786440 | tf_op jit(solution)/shard_map/ppermute | solution.py:264
  8.8 1.5 %collective-permute-start.2 = (bf16[128,1024]{1,0:T(8,128)(2,1)}, bf16[128,1024]{1,0:T(8,128)(2,1)S(1)}, u32[]{:S(2)}, u32[]{:S(2)}) collective-permute-start(bf16[128,1024]{1,0:T(8,128)(2,1)} %get-tuple-element.16), channel_id=1, source_target_pairs={{0,2},{1,3},{2,0},{3,1},{4,6},{5,7},{6,4},{7,5},{8,10},{9,11},{10,... | collective-permute-start | bytes 786440 | tf_op jit(solution)/shard_map/ppermute | solution.py:264
  10.3 1.6 %collective-permute-start = (bf16[128,4224]{1,0:T(8,128)(2,1)}, bf16[128,4224]{1,0:T(8,128)(2,1)S(1)}, u32[]{:S(2)}, u32[]{:S(2)}) collective-permute-start(bf16[128,4224]{1,0:T(8,128)(2,1)} %get-tuple-element.14), channel_id=1, source_target_pairs={{0,8},{8,16},{16,24},{24,0},{1,9},{9,17},{17,25},{25,1},{2,10},{10... | collective-permute-start | bytes 3244040 | tf_op jit(solution)/shard_map/ppermute | solution.py:278
  11.9 1.0 %slice_bitcast_fusion.28 = (bf16[1,128,256]{2,1,0:T(8,128)(2,1)S(1)}, bf16[1,128,256]{2,1,0:T(8,128)(2,1)S(1)}, bf16[1,128,256]{2,1,0:T(8,128)(2,1)S(1)}, bf16[1,128,256]{2,1,0:T(8,128)(2,1)S(1)}) fusion(bf16[128,1024]{1,0:T(8,128)(2,1)} %get-tuple-element.16), kind=kLoop, calls=%fused_computation.41 | loop fusion | bytes 524288 | tf_op jit(solution)/shard_map/stack | solution.py:284
  12.8 0.5 collective-permute-done.1
  13.3 3.5 %collective-permute-start.4 = (bf16[128,1024]{1,0:T(8,128)(2,1)}, bf16[128,1024]{1,0:T(8,128)(2,1)S(1)}, u32[]{:S(2)}, u32[]{:S(2)}) collective-permute-start(bf16[128,1024]{1,0:T(8,128)(2,1)} %get-tuple-element.16), channel_id=1, source_target_pairs={{0,6},{1,7},{2,4},{3,5},{4,2},{5,3},{6,0},{7,1},{8,14},{9,15},{10,... | collective-permute-start | bytes 786440 | tf_op jit(solution)/shard_map/ppermute | solution.py:264
  16.9 5.1 %collective-permute-done.4 = bf16[128,1024]{1,0:T(8,128)(2,1)S(1)} collective-permute-done((bf16[128,1024]{1,0:T(8,128)(2,1)}, bf16[128,1024]{1,0:T(8,128)(2,1)S(1)}, u32[]{:S(2)}, u32[]{:S(2)}) %collective-permute-start.4) | collective-permute-done | bytes 262176 | tf_op jit(solution)/shard_map/ppermute | solution.py:264
  22.2 0.6 collective-permute-start.9
  23.0 0.6 collective-permute-start.7
  23.5 0.1 maximum_maximum_fusion.mine
  23.7 1.6 %collective-permute-start.6 = (bf16[128,1024]{1,0:T(8,128)(2,1)S(1)}, bf16[128,1024]{1,0:T(8,128)(2,1)S(1)}, u32[]{:S(2)}, u32[]{:S(2)}) collective-permute-start(bf16[128,1024]{1,0:T(8,128)(2,1)S(1)} %collective-permute-done.1), channel_id=1, source_target_pairs={{0,4},{1,5},{2,6},{3,7},{4,0},{5,1},{6,2},{7,3},{8,12},{9,13},{10,... | collective-permute-start | bytes 786440 | tf_op jit(solution)/shard_map/ppermute | solution.py:264
  25.3 1.5 %collective-permute-start.5 = (bf16[128,1024]{1,0:T(8,128)(2,1)S(1)}, bf16[128,1024]{1,0:T(8,128)(2,1)S(1)}, u32[]{:S(2)}, u32[]{:S(2)}) collective-permute-start(bf16[128,1024]{1,0:T(8,128)(2,1)S(1)} %collective-permute-done.1), channel_id=1, source_target_pairs={{0,2},{1,3},{2,0},{3,1},{4,6},{5,7},{6,4},{7,5},{8,10},{9,11},{10,... | collective-permute-start | bytes 786440 | tf_op jit(solution)/shard_map/ppermute | solution.py:264
  26.8 0.1 pad_maximum_fusion.theirs
  27.0 3.8 %shard_map.57 = bf16[128,4096]{1,0:T(8,128)(2,1)S(1)} custom-call(s32[8,8]{1,0:T(8,128)S(1)} %bitcast.77, s32[8]{0:T(128)S(1)} %bitcast.79, bf16[128,8192]{1,0:T(8,128)(2,1)S(1)} %bitcast.75, bf16[4,128,1024]{2,1,0:T(8,128)(2,1)S(1)} %maximum_maximum_fusion.mine, bf16[4,128,1024]{2,1,0:T(8,128)(2,1)S(1)} %pad_maximum_fusion.theirs), custom_call_target="tpu_custom_call" | custom-call | flops 1 | bytes 1 | tf_op jit(solution)/shard_map/pallas_call | solution.py:174
  30.8 1.6 %collective-permute-start.16 = (bf16[128,4096]{1,0:T(8,128)(2,1)S(1)}, bf16[128,4096]{1,0:T(8,128)(2,1)S(1)}, u32[]{:S(2)}, u32[]{:S(2)}) collective-permute-start(bf16[128,4096]{1,0:T(8,128)(2,1)S(1)} %shard_map.57), channel_id=1, source_target_pairs={{0,8},{8,16},{16,24},{24,0},{1,9},{9,17},{17,25},{25,1},{2,10},{10... | collective-permute-start | bytes 3145736 | tf_op jit(solution)/shard_map/ppermute | solution.py:278
  32.4 6.7 %collective-permute-done.q_ref = bf16[128,4224]{1,0:T(8,128)(2,1)S(1)} collective-permute-done((bf16[128,4224]{1,0:T(8,128)(2,1)}, bf16[128,4224]{1,0:T(8,128)(2,1)S(1)}, u32[]{:S(2)}, u32[]{:S(2)}) %collective-permute-start) | collective-permute-done | bytes 1081376 | tf_op jit(solution)/shard_map/ppermute | solution.py:278
  39.1 7.2 %collective-permute-done.11 = bf16[128,1024]{1,0:T(8,128)(2,1)S(1)} collective-permute-done((bf16[128,1024]{1,0:T(8,128)(2,1)S(1)}, bf16[128,1024]{1,0:T(8,128)(2,1)S(1)}, u32[]{:S(2)}, u32[]{:S(2)}) %collective-permute-start.11) | collective-permute-done | bytes 262176 | tf_op jit(solution)/shard_map/ppermute | solution.py:264
  46.6 0.5 collective-permute-start.14
  47.2 0.4 collective-permute-start.12
  47.6 0.1 pad_maximum_fusion.1.mine
  47.8 0.4 collective-permute-done.15
  48.1 0.4 collective-permute-done.14
  48.5 0.4 collective-permute-done.13
  48.9 0.4 collective-permute-done.12
  49.3 0.1 pad_maximum_fusion.2.theirs
  49.4 3.8 %shard_map.58 = bf16[128,4096]{1,0:T(8,128)(2,1)S(1)} custom-call(s32[8,8]{1,0:T(8,128)S(1)} %slice.143.mask, s32[8]{0:T(128)S(1)} %slice_bitcast_fusion.32.live, bf16[128,4224]{1,0:T(8,128)(2,1)S(1)} %collective-permute-done.q_ref, bf16[4,128,1024]{2,1,0:T(8,128)(2,1)S(1)} %pad_maximum_fusion.1.mine, bf16[4,128,1024]{2,1,0:T(8,128)(2,1)S(1)} %pad_maximum_fusion.2.theirs), custom_call_target="tpu_custom_call" | custom-call | flops 1 | bytes 1 | tf_op jit(solution)/shard_map/pallas_call | solution.py:174
  53.2 1.5 %concatenate.19 = bf16[128,8192]{1,0:T(8,128)(2,1)} pad(bf16[128,4096]{1,0:T(8,128)(2,1)S(1)} %shard_map.58, bf16[]{:T(256)} %constant.1.clone.1), padding=0_0x0_4096 | pad | bytes 3145730 | tf_op jit(solution)/shard_map/concatenate | solution.py:309
  54.7 4.8 %collective-permute-done.16 = bf16[128,4096]{1,0:T(8,128)(2,1)S(1)} collective-permute-done((bf16[128,4096]{1,0:T(8,128)(2,1)S(1)}, bf16[128,4096]{1,0:T(8,128)(2,1)S(1)}, u32[]{:S(2)}, u32[]{:S(2)}) %collective-permute-start.16) | collective-permute-done | bytes 1048608 | tf_op jit(solution)/shard_map/ppermute | solution.py:278
  59.5 1.0 %bitcast_dynamic-update-slice_fusion = bf16[1,128,8192]{2,1,0:T(8,128)(2,1)} fusion(bf16[1,128,8192]{2,1,0:T(8,128)(2,1)} %bitcast.80, bf16[128,4096]{1,0:T(8,128)(2,1)S(1)} %collective-permute-done.16), kind=kLoop, calls=%fused_computation.4 | loop fusion | bytes 2097152 | tf_op jit(solution)/shard_map/dynamic_update_slice | solution.py:310
  (35 shorter events, 0.8 us)
Async XLA Ops:
  1.7 11.6 %collective-permute-start.1 = (bf16[128,1024]{1,0:T(8,128)(2,1)}, bf16[128,1024]{1,0:T(8,128)(2,1)S(1)}, u32[]{:S(2)}, u32[]{:S(2)}) collective-permute-start(bf16[128,1024]{1,0:T(8,128)(2,1)} %shard_map.55.sent), channel_id=1, source_target_pairs={{0,8},{8,16},{16,24},{24,0},{1,9},{9,17},{17,25},{25,1},{2,10},{10... | collective-permute-start | bytes 786440 | tf_op jit(solution)/shard_map/ppermute | solution.py:278
  7.3 9.6 %collective-permute-start.3 = (bf16[128,1024]{1,0:T(8,128)(2,1)}, bf16[128,1024]{1,0:T(8,128)(2,1)S(1)}, u32[]{:S(2)}, u32[]{:S(2)}) collective-permute-start(bf16[128,1024]{1,0:T(8,128)(2,1)} %get-tuple-element.16), channel_id=1, source_target_pairs={{0,4},{1,5},{2,6},{3,7},{4,0},{5,1},{6,2},{7,3},{8,12},{9,13},{10,... | collective-permute-start | bytes 786440 | tf_op jit(solution)/shard_map/ppermute | solution.py:264
  8.8 8.1 %collective-permute-start.2 = (bf16[128,1024]{1,0:T(8,128)(2,1)}, bf16[128,1024]{1,0:T(8,128)(2,1)S(1)}, u32[]{:S(2)}, u32[]{:S(2)}) collective-permute-start(bf16[128,1024]{1,0:T(8,128)(2,1)} %get-tuple-element.16), channel_id=1, source_target_pairs={{0,2},{1,3},{2,0},{3,1},{4,6},{5,7},{6,4},{7,5},{8,10},{9,11},{10,... | collective-permute-start | bytes 786440 | tf_op jit(solution)/shard_map/ppermute | solution.py:264
  10.3 28.8 %collective-permute-start = (bf16[128,4224]{1,0:T(8,128)(2,1)}, bf16[128,4224]{1,0:T(8,128)(2,1)S(1)}, u32[]{:S(2)}, u32[]{:S(2)}) collective-permute-start(bf16[128,4224]{1,0:T(8,128)(2,1)} %get-tuple-element.14), channel_id=1, source_target_pairs={{0,8},{8,16},{16,24},{24,0},{1,9},{9,17},{17,25},{25,1},{2,10},{10... | collective-permute-start | bytes 3244040 | tf_op jit(solution)/shard_map/ppermute | solution.py:278
  13.3 8.7 %collective-permute-start.4 = (bf16[128,1024]{1,0:T(8,128)(2,1)}, bf16[128,1024]{1,0:T(8,128)(2,1)S(1)}, u32[]{:S(2)}, u32[]{:S(2)}) collective-permute-start(bf16[128,1024]{1,0:T(8,128)(2,1)} %get-tuple-element.16), channel_id=1, source_target_pairs={{0,6},{1,7},{2,4},{3,5},{4,2},{5,3},{6,0},{7,1},{8,14},{9,15},{10,... | collective-permute-start | bytes 786440 | tf_op jit(solution)/shard_map/ppermute | solution.py:264
  22.1 1.6 %collective-permute-start.10 = (bf16[4,128,256]{2,1,0:T(8,128)(2,1)S(1)}, bf16[4,128,256]{2,1,0:T(8,128)(2,1)S(1)}, u32[]{:S(2)}, u32[]{:S(2)}) collective-permute-start(bf16[4,128,256]{2,1,0:T(8,128)(2,1)S(1)} %pad_maximum_fusion.6), channel_id=1, source_target_pairs={{0,1},{1,0},{2,3},{3,2},{4,5},{5,4},{6,7},{7,6},{8,9},{9,8},{10,11... | collective-permute-start | bytes 786440 | tf_op jit(solution)/shard_map/ppermute | solution.py:264
  22.2 3.1 %collective-permute-start.9 = (bf16[4,128,256]{2,1,0:T(8,128)(2,1)S(1)}, bf16[4,128,256]{2,1,0:T(8,128)(2,1)S(1)}, u32[]{:S(2)}, u32[]{:S(2)}) collective-permute-start(bf16[4,128,256]{2,1,0:T(8,128)(2,1)S(1)} %pad_maximum_fusion.5), channel_id=1, source_target_pairs={{0,1},{1,0},{2,3},{3,2},{4,5},{5,4},{6,7},{7,6},{8,9},{9,8},{10,11... | collective-permute-start | bytes 786440 | tf_op jit(solution)/shard_map/ppermute | solution.py:264
  22.8 4.0 %collective-permute-start.8 = (bf16[4,128,256]{2,1,0:T(8,128)(2,1)S(1)}, bf16[4,128,256]{2,1,0:T(8,128)(2,1)S(1)}, u32[]{:S(2)}, u32[]{:S(2)}) collective-permute-start(bf16[4,128,256]{2,1,0:T(8,128)(2,1)S(1)} %pad_maximum_fusion.4), channel_id=1, source_target_pairs={{0,1},{1,0},{2,3},{3,2},{4,5},{5,4},{6,7},{7,6},{8,9},{9,8},{10,11... | collective-permute-start | bytes 786440 | tf_op jit(solution)/shard_map/ppermute | solution.py:264
  22.9 4.0 %copy-start = (bf16[1,128,8192]{2,1,0:T(8,128)(2,1)S(1)}, bf16[1,128,8192]{2,1,0:T(8,128)(2,1)}, u32[]{:S(2)}) copy-start(bf16[1,128,8192]{2,1,0:T(8,128)(2,1)} %param.5) | copy-start | bytes 6291460
  23.0 4.0 %copy-start.1 = (s32[1,8,8]{2,1,0:T(8,128)S(1)}, s32[1,8,8]{2,1,0:T(8,128)}, u32[]{:S(2)}) copy-start(s32[1,8,8]{2,1,0:T(8,128)} %param.8) | copy-start | bytes 772
  23.0 4.0 %copy-start.2 = (s32[1,8]{1,0:T(1,128)S(1)}, s32[1,8]{1,0:T(1,128)}, u32[]{:S(2)}) copy-start(s32[1,8]{1,0:T(1,128)} %param.9) | copy-start | bytes 100
  23.0 3.8 %collective-permute-start.7 = (bf16[4,128,256]{2,1,0:T(8,128)(2,1)S(1)}, bf16[4,128,256]{2,1,0:T(8,128)(2,1)S(1)}, u32[]{:S(2)}, u32[]{:S(2)}) collective-permute-start(bf16[4,128,256]{2,1,0:T(8,128)(2,1)S(1)} %pad_maximum_fusion.3), channel_id=1, source_target_pairs={{0,1},{1,0},{2,3},{3,2},{4,5},{5,4},{6,7},{7,6},{8,9},{9,8},{10,11... | collective-permute-start | bytes 786440 | tf_op jit(solution)/shard_map/ppermute | solution.py:264
  23.7 8.7 %collective-permute-start.6 = (bf16[128,1024]{1,0:T(8,128)(2,1)S(1)}, bf16[128,1024]{1,0:T(8,128)(2,1)S(1)}, u32[]{:S(2)}, u32[]{:S(2)}) collective-permute-start(bf16[128,1024]{1,0:T(8,128)(2,1)S(1)} %collective-permute-done.1), channel_id=1, source_target_pairs={{0,4},{1,5},{2,6},{3,7},{4,0},{5,1},{6,2},{7,3},{8,12},{9,13},{10,... | collective-permute-start | bytes 786440 | tf_op jit(solution)/shard_map/ppermute | solution.py:264
  25.3 13.8 %collective-permute-start.5 = (bf16[128,1024]{1,0:T(8,128)(2,1)S(1)}, bf16[128,1024]{1,0:T(8,128)(2,1)S(1)}, u32[]{:S(2)}, u32[]{:S(2)}) collective-permute-start(bf16[128,1024]{1,0:T(8,128)(2,1)S(1)} %collective-permute-done.1), channel_id=1, source_target_pairs={{0,2},{1,3},{2,0},{3,1},{4,6},{5,7},{6,4},{7,5},{8,10},{9,11},{10,... | collective-permute-start | bytes 786440 | tf_op jit(solution)/shard_map/ppermute | solution.py:264
  30.8 28.7 %collective-permute-start.16 = (bf16[128,4096]{1,0:T(8,128)(2,1)S(1)}, bf16[128,4096]{1,0:T(8,128)(2,1)S(1)}, u32[]{:S(2)}, u32[]{:S(2)}) collective-permute-start(bf16[128,4096]{1,0:T(8,128)(2,1)S(1)} %shard_map.57), channel_id=1, source_target_pairs={{0,8},{8,16},{16,24},{24,0},{1,9},{9,17},{17,25},{25,1},{2,10},{10... | collective-permute-start | bytes 3145736 | tf_op jit(solution)/shard_map/ppermute | solution.py:278
  39.1 7.3 %collective-permute-start.11 = (bf16[128,1024]{1,0:T(8,128)(2,1)S(1)}, bf16[128,1024]{1,0:T(8,128)(2,1)S(1)}, u32[]{:S(2)}, u32[]{:S(2)}) collective-permute-start(bf16[128,1024]{1,0:T(8,128)(2,1)S(1)} %collective-permute-done.1), channel_id=1, source_target_pairs={{0,6},{1,7},{2,4},{3,5},{4,2},{5,3},{6,0},{7,1},{8,14},{9,15},{10,... | collective-permute-start | bytes 786440 | tf_op jit(solution)/shard_map/ppermute | solution.py:264
  46.5 1.6 %collective-permute-start.15 = (bf16[4,128,256]{2,1,0:T(8,128)(2,1)S(1)}, bf16[4,128,256]{2,1,0:T(8,128)(2,1)S(1)}, u32[]{:S(2)}, u32[]{:S(2)}) collective-permute-start(bf16[4,128,256]{2,1,0:T(8,128)(2,1)S(1)} %get-tuple-element.22), channel_id=1, source_target_pairs={{0,1},{1,0},{2,3},{3,2},{4,5},{5,4},{6,7},{7,6},{8,9},{9,8},{10,11... | collective-permute-start | bytes 786440 | tf_op jit(solution)/shard_map/ppermute | solution.py:264
  46.6 1.9 %collective-permute-start.14 = (bf16[4,128,256]{2,1,0:T(8,128)(2,1)S(1)}, bf16[4,128,256]{2,1,0:T(8,128)(2,1)S(1)}, u32[]{:S(2)}, u32[]{:S(2)}) collective-permute-start(bf16[4,128,256]{2,1,0:T(8,128)(2,1)S(1)} %get-tuple-element.21), channel_id=1, source_target_pairs={{0,1},{1,0},{2,3},{3,2},{4,5},{5,4},{6,7},{7,6},{8,9},{9,8},{10,11... | collective-permute-start | bytes 786440 | tf_op jit(solution)/shard_map/ppermute | solution.py:264
  47.1 1.8 %collective-permute-start.13 = (bf16[4,128,256]{2,1,0:T(8,128)(2,1)S(1)}, bf16[4,128,256]{2,1,0:T(8,128)(2,1)S(1)}, u32[]{:S(2)}, u32[]{:S(2)}) collective-permute-start(bf16[4,128,256]{2,1,0:T(8,128)(2,1)S(1)} %get-tuple-element.20), channel_id=1, source_target_pairs={{0,1},{1,0},{2,3},{3,2},{4,5},{5,4},{6,7},{7,6},{8,9},{9,8},{10,11... | collective-permute-start | bytes 786440 | tf_op jit(solution)/shard_map/ppermute | solution.py:264
  47.2 2.1 %collective-permute-start.12 = (bf16[4,128,256]{2,1,0:T(8,128)(2,1)S(1)}, bf16[4,128,256]{2,1,0:T(8,128)(2,1)S(1)}, u32[]{:S(2)}, u32[]{:S(2)}) collective-permute-start(bf16[4,128,256]{2,1,0:T(8,128)(2,1)S(1)} %get-tuple-element.19), channel_id=1, source_target_pairs={{0,1},{1,0},{2,3},{3,2},{4,5},{5,4},{6,7},{7,6},{8,9},{9,8},{10,11... | collective-permute-start | bytes 786440 | tf_op jit(solution)/shard_map/ppermute | solution.py:264

commit v2 on v1

--- a/solution.py
+++ b/solution.py
@@ -207,20 +207,24 @@
     )(keys, values)
 
 
-def rest_kernel(first, mask, live, q_ref, k_ref, v_ref, sent, q_sent, part):
+def rest_kernel(first, mask, live, k_ref, v_ref, sent, *refs):
+    q_refs, (q_sent, part) = refs[:-2], refs[-2:]
     pack_heads(k_ref, v_ref, first, part, part.shape[1] // (2 * HEAD_SIZE))
-    last = q_ref.shape[1]
-    q_sent[:, :last] = q_ref[...]
+    step = q_refs[0].shape[1]
+    last = step * len(q_refs)
+    for i, ref in enumerate(q_refs):
+        q_sent[:, i * step : (i + 1) * step] = ref[...]
     q_sent[:, last:] = jnp.zeros_like(q_sent[:, last:])
     blocks = live.shape[0]
     deep = 16
     row = lax.broadcasted_iota(jnp.int32, (deep, HEAD_SIZE), 0)
     col = lax.broadcasted_iota(jnp.int32, (deep, HEAD_SIZE), 1)
+    place = jnp.where(col < blocks, row * blocks + col, -1)
     tile = jnp.zeros((deep, HEAD_SIZE), jnp.int32)
     for j in range(blocks):
-        tile = jnp.where((row == blocks) & (col == j), live[j], tile)
+        tile = jnp.where(place == blocks * blocks + j, live[j], tile)
         for i in range(blocks):
-            tile = jnp.where((row == i) & (col == j), mask[i, j], tile)
+            tile = jnp.where(place == i * blocks + j, mask[i, j], tile)
     q_sent[:deep, last:] = tile.astype(jnp.float32).astype(q_sent.dtype)
 
 
@@ -237,11 +241,12 @@
         functools.partial(rest_kernel, first),
         grid=(1,),
         out_shape=[jax.ShapeDtypeStruct(shape, keys.dtype) for shape in shapes],
-        in_specs=[smem, smem, whole((rows, q_cols)), whole(keys.shape), whole(values.shape)]
-        + [pl.BlockSpec(memory_space=pl.ANY)],
+        in_specs=[smem, smem, whole(keys.shape), whole(values.shape)]
+        + [pl.BlockSpec(memory_space=pl.ANY)]
+        + [pl.BlockSpec((rows, q_cols // first), lambda i, at=at: (0, at)) for at in range(first)],
         out_specs=[whole(shape) for shape in shapes],
         cost_estimate=COST,
-    )(mask, live, queries, keys, values, sent)
+    )(mask, live, keys, values, sent, *[queries] * first)
 
 
 def pack_pairs(keys, values, heads):

time: 60.8 us -> 60.8 us (level)
  no operation moved by 1% of the time
where the time goes in v2:
time: 60.8 us; the launch traced here: 60.6 us
  waiting for transfers between devices  25.8 us (42%)
  starting transfers between devices  18.2 us (30%)
  Pallas kernels  11.9 us (20%)
  local copies, waits for them, and re-layouts  3.66 us (6%)
  other arithmetic  0.81 us (1%)
    ppermute x14, waiting for transfers between devices, exchange(): lax.ppermute(part, ('section', 'seq'), on_plane(nsec, lambda i: i ^ by))  13.9 us
    ppermute x14, starting transfers between devices, exchange(): lax.ppermute(part, ('section', 'seq'), on_plane(nsec, lambda i: i ^ by))  12 us
    ppermute x3, waiting for transfers between devices, on(): return lax.ppermute(value, 'section', onward)  11.9 us
    pallas_call x2, Pallas kernels, attend_planar(): pl.pallas_call(functools.partial(planar_kernel, HEAD_SIZE ** (-0.5) * 1.4...  7.62 us
    ppermute x3, starting transfers between devices, on(): return lax.ppermute(value, 'section', onward)  6.23 us
    pallas_call x1, Pallas kernels, pack_rest(): pl.pallas_call(functools.partial(rest_kernel, first), grid=(1,), out_shap...  2.51 us
    pallas_call x1, Pallas kernels, pack_ahead(): pl.pallas_call(ahead_kernel, grid=(1,), out_shape=jax.ShapeDtypeStruct(sh...  1.74 us
    concatenate x1, local copies, waits for them, and re-layouts, per_device_8(): held = jnp.concatenate(first + [jnp.zeros_like(out)], axis=1)  1.51 us
  transfers between devices with their start and end apart: 17, of which 9 were waited for; matrix products, arithmetic and copies ran while one was open for 6% of the time, Pallas kernels for 17%

profile of v2, /device:TPU:0, one launch (start us, length us, event | category | flops | bytes accessed | tf_op | source)
XLA Modules:
  0.0 60.6 jit_solution(2207973521299740950)
XLA Ops:
  0.0 1.7 %shard_map.55.sent = bf16[128,1024]{1,0:T(8,128)(2,1)} custom-call(bf16[128,1024]{1,0:T(8,128)(2,1)} %bitcast.84, bf16[128,1024]{1,0:T(8,128)(2,1)} %bitcast.86), custom_call_target="tpu_custom_call" | custom-call | flops 1 | bytes 1 | tf_op jit(solution)/shard_map/pallas_call | solution.py:200
  1.7 3.0 %collective-permute-start.1 = (bf16[128,1024]{1,0:T(8,128)(2,1)}, bf16[128,1024]{1,0:T(8,128)(2,1)S(1)}, u32[]{:S(2)}, u32[]{:S(2)}) collective-permute-start(bf16[128,1024]{1,0:T(8,128)(2,1)} %shard_map.55.sent), channel_id=1, source_target_pairs={{0,8},{8,16},{16,24},{24,0},{1,9},{9,17},{17,25},{25,1},{2,10},{10... | collective-permute-start | bytes 786440 | tf_op jit(solution)/shard_map/ppermute | solution.py:283
  4.8 2.5 %shard_map.56 = (bf16[128,4224]{1,0:T(8,128)(2,1)}, bf16[128,1024]{1,0:T(8,128)(2,1)}) custom-call(s32[8,8]{1,0:T(8,128)} %bitcast.79, s32[8]{0:T(128)} %bitcast.81, bf16[128,1024]{1,0:T(8,128)(2,1)} %bitcast.85, bf16[128,1024]{1,0:T(8,128)(2,1)} %bitcast.87, bf16[128,1024]{1,0:T(8,128)(2,1)} %shard_map.55.sent, bf16[128,8192]{1,0:T(8,128)(2,1)} %bitcast.74, ...), custom_call_target="tpu_custom_call" | custom-call | flops 1 | bytes 1 | tf_op jit(solution)/shard_map/pallas_call | solution.py:240
  7.3 1.5 %collective-permute-start.3 = (bf16[128,1024]{1,0:T(8,128)(2,1)}, bf16[128,1024]{1,0:T(8,128)(2,1)S(1)}, u32[]{:S(2)}, u32[]{:S(2)}) collective-permute-start(bf16[128,1024]{1,0:T(8,128)(2,1)} %get-tuple-element.16), channel_id=1, source_target_pairs={{0,4},{1,5},{2,6},{3,7},{4,0},{5,1},{6,2},{7,3},{8,12},{9,13},{10,... | collective-permute-start | bytes 786440 | tf_op jit(solution)/shard_map/ppermute | solution.py:269
  8.8 1.5 %collective-permute-start.2 = (bf16[128,1024]{1,0:T(8,128)(2,1)}, bf16[128,1024]{1,0:T(8,128)(2,1)S(1)}, u32[]{:S(2)}, u32[]{:S(2)}) collective-permute-start(bf16[128,1024]{1,0:T(8,128)(2,1)} %get-tuple-element.16), channel_id=1, source_target_pairs={{0,2},{1,3},{2,0},{3,1},{4,6},{5,7},{6,4},{7,5},{8,10},{9,11},{10,... | collective-permute-start | bytes 786440 | tf_op jit(solution)/shard_map/ppermute | solution.py:269
  10.3 1.6 %collective-permute-start = (bf16[128,4224]{1,0:T(8,128)(2,1)}, bf16[128,4224]{1,0:T(8,128)(2,1)S(1)}, u32[]{:S(2)}, u32[]{:S(2)}) collective-permute-start(bf16[128,4224]{1,0:T(8,128)(2,1)} %get-tuple-element.14), channel_id=1, source_target_pairs={{0,8},{8,16},{16,24},{24,0},{1,9},{9,17},{17,25},{25,1},{2,10},{10... | collective-permute-start | bytes 3244040 | tf_op jit(solution)/shard_map/ppermute | solution.py:283
  11.9 1.0 %slice_bitcast_fusion.28 = (bf16[1,128,256]{2,1,0:T(8,128)(2,1)S(1)}, bf16[1,128,256]{2,1,0:T(8,128)(2,1)S(1)}, bf16[1,128,256]{2,1,0:T(8,128)(2,1)S(1)}, bf16[1,128,256]{2,1,0:T(8,128)(2,1)S(1)}) fusion(bf16[128,1024]{1,0:T(8,128)(2,1)} %get-tuple-element.16), kind=kLoop, calls=%fused_computation.41 | loop fusion | bytes 524288 | tf_op jit(solution)/shard_map/stack | solution.py:289
  12.8 0.5 collective-permute-done.1
  13.3 3.5 %collective-permute-start.4 = (bf16[128,1024]{1,0:T(8,128)(2,1)}, bf16[128,1024]{1,0:T(8,128)(2,1)S(1)}, u32[]{:S(2)}, u32[]{:S(2)}) collective-permute-start(bf16[128,1024]{1,0:T(8,128)(2,1)} %get-tuple-element.16), channel_id=1, source_target_pairs={{0,6},{1,7},{2,4},{3,5},{4,2},{5,3},{6,0},{7,1},{8,14},{9,15},{10,... | collective-permute-start | bytes 786440 | tf_op jit(solution)/shard_map/ppermute | solution.py:269
  16.9 5.2 %collective-permute-done.4 = bf16[128,1024]{1,0:T(8,128)(2,1)S(1)} collective-permute-done((bf16[128,1024]{1,0:T(8,128)(2,1)}, bf16[128,1024]{1,0:T(8,128)(2,1)S(1)}, u32[]{:S(2)}, u32[]{:S(2)}) %collective-permute-start.4) | collective-permute-done | bytes 262176 | tf_op jit(solution)/shard_map/ppermute | solution.py:269
  22.2 0.6 collective-permute-start.9
  23.0 0.6 collective-permute-start.7
  23.6 0.1 maximum_maximum_fusion.mine
  23.7 1.6 %collective-permute-start.6 = (bf16[128,1024]{1,0:T(8,128)(2,1)S(1)}, bf16[128,1024]{1,0:T(8,128)(2,1)S(1)}, u32[]{:S(2)}, u32[]{:S(2)}) collective-permute-start(bf16[128,1024]{1,0:T(8,128)(2,1)S(1)} %collective-permute-done.1), channel_id=1, source_target_pairs={{0,4},{1,5},{2,6},{3,7},{4,0},{5,1},{6,2},{7,3},{8,12},{9,13},{10,... | collective-permute-start | bytes 786440 | tf_op jit(solution)/shard_map/ppermute | solution.py:269
  25.3 1.5 %collective-permute-start.5 = (bf16[128,1024]{1,0:T(8,128)(2,1)S(1)}, bf16[128,1024]{1,0:T(8,128)(2,1)S(1)}, u32[]{:S(2)}, u32[]{:S(2)}) collective-permute-start(bf16[128,1024]{1,0:T(8,128)(2,1)S(1)} %collective-permute-done.1), channel_id=1, source_target_pairs={{0,2},{1,3},{2,0},{3,1},{4,6},{5,7},{6,4},{7,5},{8,10},{9,11},{10,... | collective-permute-start | bytes 786440 | tf_op jit(solution)/shard_map/ppermute | solution.py:269
  26.8 0.1 pad_maximum_fusion.theirs
  27.0 3.8 %shard_map.57 = bf16[128,4096]{1,0:T(8,128)(2,1)S(1)} custom-call(s32[8,8]{1,0:T(8,128)S(1)} %bitcast.80, s32[8]{0:T(128)S(1)} %bitcast.82, bf16[128,8192]{1,0:T(8,128)(2,1)S(1)} %bitcast.78, bf16[4,128,1024]{2,1,0:T(8,128)(2,1)S(1)} %maximum_maximum_fusion.mine, bf16[4,128,1024]{2,1,0:T(8,128)(2,1)S(1)} %pad_maximum_fusion.theirs), custom_call_target="tpu_custom_call" | custom-call | flops 1 | bytes 1 | tf_op jit(solution)/shard_map/pallas_call | solution.py:174
  30.8 1.6 %collective-permute-start.16 = (bf16[128,4096]{1,0:T(8,128)(2,1)S(1)}, bf16[128,4096]{1,0:T(8,128)(2,1)S(1)}, u32[]{:S(2)}, u32[]{:S(2)}) collective-permute-start(bf16[128,4096]{1,0:T(8,128)(2,1)S(1)} %shard_map.57), channel_id=1, source_target_pairs={{0,8},{8,16},{16,24},{24,0},{1,9},{9,17},{17,25},{25,1},{2,10},{10... | collective-permute-start | bytes 3145736 | tf_op jit(solution)/shard_map/ppermute | solution.py:283
  32.4 6.7 %collective-permute-done.q_ref = bf16[128,4224]{1,0:T(8,128)(2,1)S(1)} collective-permute-done((bf16[128,4224]{1,0:T(8,128)(2,1)}, bf16[128,4224]{1,0:T(8,128)(2,1)S(1)}, u32[]{:S(2)}, u32[]{:S(2)}) %collective-permute-start) | collective-permute-done | bytes 1081376 | tf_op jit(solution)/shard_map/ppermute | solution.py:283
  39.1 7.2 %collective-permute-done.11 = bf16[128,1024]{1,0:T(8,128)(2,1)S(1)} collective-permute-done((bf16[128,1024]{1,0:T(8,128)(2,1)S(1)}, bf16[128,1024]{1,0:T(8,128)(2,1)S(1)}, u32[]{:S(2)}, u32[]{:S(2)}) %collective-permute-start.11) | collective-permute-done | bytes 262176 | tf_op jit(solution)/shard_map/ppermute | solution.py:269
  46.6 0.5 collective-permute-start.14
  47.2 0.4 collective-permute-start.12
  47.6 0.1 pad_maximum_fusion.1.mine
  47.8 0.4 collective-permute-done.15
  48.1 0.4 collective-permute-done.14
  48.5 0.4 collective-permute-done.13
  48.9 0.4 collective-permute-done.12
  49.3 0.1 pad_maximum_fusion.2.theirs
  49.4 3.8 %shard_map.58 = bf16[128,4096]{1,0:T(8,128)(2,1)S(1)} custom-call(s32[8,8]{1,0:T(8,128)S(1)} %slice.143.mask, s32[8]{0:T(128)S(1)} %slice_bitcast_fusion.32.live, bf16[128,4224]{1,0:T(8,128)(2,1)S(1)} %collective-permute-done.q_ref, bf16[4,128,1024]{2,1,0:T(8,128)(2,1)S(1)} %pad_maximum_fusion.1.mine, bf16[4,128,1024]{2,1,0:T(8,128)(2,1)S(1)} %pad_maximum_fusion.2.theirs), custom_call_target="tpu_custom_call" | custom-call | flops 1 | bytes 1 | tf_op jit(solution)/shard_map/pallas_call | solution.py:174
  53.2 1.5 %concatenate.19 = bf16[128,8192]{1,0:T(8,128)(2,1)} pad(bf16[128,4096]{1,0:T(8,128)(2,1)S(1)} %shard_map.58, bf16[]{:T(256)} %constant.1.clone.1), padding=0_0x0_4096 | pad | bytes 3145730 | tf_op jit(solution)/shard_map/concatenate | solution.py:314
  54.8 4.8 %collective-permute-done.16 = bf16[128,4096]{1,0:T(8,128)(2,1)S(1)} collective-permute-done((bf16[128,4096]{1,0:T(8,128)(2,1)S(1)}, bf16[128,4096]{1,0:T(8,128)(2,1)S(1)}, u32[]{:S(2)}, u32[]{:S(2)}) %collective-permute-start.16) | collective-permute-done | bytes 1048608 | tf_op jit(solution)/shard_map/ppermute | solution.py:283
  59.5 1.0 %bitcast_dynamic-update-slice_fusion = bf16[1,128,8192]{2,1,0:T(8,128)(2,1)} fusion(bf16[1,128,8192]{2,1,0:T(8,128)(2,1)} %bitcast.83, bf16[128,4096]{1,0:T(8,128)(2,1)S(1)} %collective-permute-done.16), kind=kLoop, calls=%fused_computation.4 | loop fusion | bytes 2097152 | tf_op jit(solution)/shard_map/dynamic_update_slice | solution.py:315
  (35 shorter events, 0.8 us)
Async XLA Ops:
  1.7 11.6 %collective-permute-start.1 = (bf16[128,1024]{1,0:T(8,128)(2,1)}, bf16[128,1024]{1,0:T(8,128)(2,1)S(1)}, u32[]{:S(2)}, u32[]{:S(2)}) collective-permute-start(bf16[128,1024]{1,0:T(8,128)(2,1)} %shard_map.55.sent), channel_id=1, source_target_pairs={{0,8},{8,16},{16,24},{24,0},{1,9},{9,17},{17,25},{25,1},{2,10},{10... | collective-permute-start | bytes 786440 | tf_op jit(solution)/shard_map/ppermute | solution.py:283
  7.3 9.6 %collective-permute-start.3 = (bf16[128,1024]{1,0:T(8,128)(2,1)}, bf16[128,1024]{1,0:T(8,128)(2,1)S(1)}, u32[]{:S(2)}, u32[]{:S(2)}) collective-permute-start(bf16[128,1024]{1,0:T(8,128)(2,1)} %get-tuple-element.16), channel_id=1, source_target_pairs={{0,4},{1,5},{2,6},{3,7},{4,0},{5,1},{6,2},{7,3},{8,12},{9,13},{10,... | collective-permute-start | bytes 786440 | tf_op jit(solution)/shard_map/ppermute | solution.py:269
  8.8 8.1 %collective-permute-start.2 = (bf16[128,1024]{1,0:T(8,128)(2,1)}, bf16[128,1024]{1,0:T(8,128)(2,1)S(1)}, u32[]{:S(2)}, u32[]{:S(2)}) collective-permute-start(bf16[128,1024]{1,0:T(8,128)(2,1)} %get-tuple-element.16), channel_id=1, source_target_pairs={{0,2},{1,3},{2,0},{3,1},{4,6},{5,7},{6,4},{7,5},{8,10},{9,11},{10,... | collective-permute-start | bytes 786440 | tf_op jit(solution)/shard_map/ppermute | solution.py:269
  10.3 28.8 %collective-permute-start = (bf16[128,4224]{1,0:T(8,128)(2,1)}, bf16[128,4224]{1,0:T(8,128)(2,1)S(1)}, u32[]{:S(2)}, u32[]{:S(2)}) collective-permute-start(bf16[128,4224]{1,0:T(8,128)(2,1)} %get-tuple-element.14), channel_id=1, source_target_pairs={{0,8},{8,16},{16,24},{24,0},{1,9},{9,17},{17,25},{25,1},{2,10},{10... | collective-permute-start | bytes 3244040 | tf_op jit(solution)/shard_map/ppermute | solution.py:283
  13.3 8.7 %collective-permute-start.4 = (bf16[128,1024]{1,0:T(8,128)(2,1)}, bf16[128,1024]{1,0:T(8,128)(2,1)S(1)}, u32[]{:S(2)}, u32[]{:S(2)}) collective-permute-start(bf16[128,1024]{1,0:T(8,128)(2,1)} %get-tuple-element.16), channel_id=1, source_target_pairs={{0,6},{1,7},{2,4},{3,5},{4,2},{5,3},{6,0},{7,1},{8,14},{9,15},{10,... | collective-permute-start | bytes 786440 | tf_op jit(solution)/shard_map/ppermute | solution.py:269
  22.1 1.6 %collective-permute-start.10 = (bf16[4,128,256]{2,1,0:T(8,128)(2,1)S(1)}, bf16[4,128,256]{2,1,0:T(8,128)(2,1)S(1)}, u32[]{:S(2)}, u32[]{:S(2)}) collective-permute-start(bf16[4,128,256]{2,1,0:T(8,128)(2,1)S(1)} %pad_maximum_fusion.6), channel_id=1, source_target_pairs={{0,1},{1,0},{2,3},{3,2},{4,5},{5,4},{6,7},{7,6},{8,9},{9,8},{10,11... | collective-permute-start | bytes 786440 | tf_op jit(solution)/shard_map/ppermute | solution.py:269
  22.2 3.1 %collective-permute-start.9 = (bf16[4,128,256]{2,1,0:T(8,128)(2,1)S(1)}, bf16[4,128,256]{2,1,0:T(8,128)(2,1)S(1)}, u32[]{:S(2)}, u32[]{:S(2)}) collective-permute-start(bf16[4,128,256]{2,1,0:T(8,128)(2,1)S(1)} %pad_maximum_fusion.5), channel_id=1, source_target_pairs={{0,1},{1,0},{2,3},{3,2},{4,5},{5,4},{6,7},{7,6},{8,9},{9,8},{10,11... | collective-permute-start | bytes 786440 | tf_op jit(solution)/shard_map/ppermute | solution.py:269
  22.8 4.0 %collective-permute-start.8 = (bf16[4,128,256]{2,1,0:T(8,128)(2,1)S(1)}, bf16[4,128,256]{2,1,0:T(8,128)(2,1)S(1)}, u32[]{:S(2)}, u32[]{:S(2)}) collective-permute-start(bf16[4,128,256]{2,1,0:T(8,128)(2,1)S(1)} %pad_maximum_fusion.4), channel_id=1, source_target_pairs={{0,1},{1,0},{2,3},{3,2},{4,5},{5,4},{6,7},{7,6},{8,9},{9,8},{10,11... | collective-permute-start | bytes 786440 | tf_op jit(solution)/shard_map/ppermute | solution.py:269
  23.0 4.0 %copy-start = (bf16[1,128,8192]{2,1,0:T(8,128)(2,1)S(1)}, bf16[1,128,8192]{2,1,0:T(8,128)(2,1)}, u32[]{:S(2)}) copy-start(bf16[1,128,8192]{2,1,0:T(8,128)(2,1)} %param.5) | copy-start | bytes 6291460
  23.0 4.0 %copy-start.1 = (s32[1,8,8]{2,1,0:T(8,128)S(1)}, s32[1,8,8]{2,1,0:T(8,128)}, u32[]{:S(2)}) copy-start(s32[1,8,8]{2,1,0:T(8,128)} %param.8) | copy-start | bytes 772
  23.0 4.0 %copy-start.2 = (s32[1,8]{1,0:T(1,128)S(1)}, s32[1,8]{1,0:T(1,128)}, u32[]{:S(2)}) copy-start(s32[1,8]{1,0:T(1,128)} %param.9) | copy-start | bytes 100
  23.0 3.8 %collective-permute-start.7 = (bf16[4,128,256]{2,1,0:T(8,128)(2,1)S(1)}, bf16[4,128,256]{2,1,0:T(8,128)(2,1)S(1)}, u32[]{:S(2)}, u32[]{:S(2)}) collective-permute-start(bf16[4,128,256]{2,1,0:T(8,128)(2,1)S(1)} %pad_maximum_fusion.3), channel_id=1, source_target_pairs={{0,1},{1,0},{2,3},{3,2},{4,5},{5,4},{6,7},{7,6},{8,9},{9,8},{10,11... | collective-permute-start | bytes 786440 | tf_op jit(solution)/shard_map/ppermute | solution.py:269
  23.7 8.7 %collective-permute-start.6 = (bf16[128,1024]{1,0:T(8,128)(2,1)S(1)}, bf16[128,1024]{1,0:T(8,128)(2,1)S(1)}, u32[]{:S(2)}, u32[]{:S(2)}) collective-permute-start(bf16[128,1024]{1,0:T(8,128)(2,1)S(1)} %collective-permute-done.1), channel_id=1, source_target_pairs={{0,4},{1,5},{2,6},{3,7},{4,0},{5,1},{6,2},{7,3},{8,12},{9,13},{10,... | collective-permute-start | bytes 786440 | tf_op jit(solution)/shard_map/ppermute | solution.py:269
  25.3 13.8 %collective-permute-start.5 = (bf16[128,1024]{1,0:T(8,128)(2,1)S(1)}, bf16[128,1024]{1,0:T(8,128)(2,1)S(1)}, u32[]{:S(2)}, u32[]{:S(2)}) collective-permute-start(bf16[128,1024]{1,0:T(8,128)(2,1)S(1)} %collective-permute-done.1), channel_id=1, source_target_pairs={{0,2},{1,3},{2,0},{3,1},{4,6},{5,7},{6,4},{7,5},{8,10},{9,11},{10,... | collective-permute-start | bytes 786440 | tf_op jit(solution)/shard_map/ppermute | solution.py:269
  30.8 28.7 %collective-permute-start.16 = (bf16[128,4096]{1,0:T(8,128)(2,1)S(1)}, bf16[128,4096]{1,0:T(8,128)(2,1)S(1)}, u32[]{:S(2)}, u32[]{:S(2)}) collective-permute-start(bf16[128,4096]{1,0:T(8,128)(2,1)S(1)} %shard_map.57), channel_id=1, source_target_pairs={{0,8},{8,16},{16,24},{24,0},{1,9},{9,17},{17,25},{25,1},{2,10},{10... | collective-permute-start | bytes 3145736 | tf_op jit(solution)/shard_map/ppermute | solution.py:283
  39.1 7.3 %collective-permute-start.11 = (bf16[128,1024]{1,0:T(8,128)(2,1)S(1)}, bf16[128,1024]{1,0:T(8,128)(2,1)S(1)}, u32[]{:S(2)}, u32[]{:S(2)}) collective-permute-start(bf16[128,1024]{1,0:T(8,128)(2,1)S(1)} %collective-permute-done.1), channel_id=1, source_target_pairs={{0,6},{1,7},{2,4},{3,5},{4,2},{5,3},{6,0},{7,1},{8,14},{9,15},{10,... | collective-permute-start | bytes 786440 | tf_op jit(solution)/shard_map/ppermute | solution.py:269
  46.5 1.6 %collective-permute-start.15 = (bf16[4,128,256]{2,1,0:T(8,128)(2,1)S(1)}, bf16[4,128,256]{2,1,0:T(8,128)(2,1)S(1)}, u32[]{:S(2)}, u32[]{:S(2)}) collective-permute-start(bf16[4,128,256]{2,1,0:T(8,128)(2,1)S(1)} %get-tuple-element.22), channel_id=1, source_target_pairs={{0,1},{1,0},{2,3},{3,2},{4,5},{5,4},{6,7},{7,6},{8,9},{9,8},{10,11... | collective-permute-start | bytes 786440 | tf_op jit(solution)/shard_map/ppermute | solution.py:269
  46.6 1.9 %collective-permute-start.14 = (bf16[4,128,256]{2,1,0:T(8,128)(2,1)S(1)}, bf16[4,128,256]{2,1,0:T(8,128)(2,1)S(1)}, u32[]{:S(2)}, u32[]{:S(2)}) collective-permute-start(bf16[4,128,256]{2,1,0:T(8,128)(2,1)S(1)} %get-tuple-element.21), channel_id=1, source_target_pairs={{0,1},{1,0},{2,3},{3,2},{4,5},{5,4},{6,7},{7,6},{8,9},{9,8},{10,11... | collective-permute-start | bytes 786440 | tf_op jit(solution)/shard_map/ppermute | solution.py:269
  47.1 1.8 %collective-permute-start.13 = (bf16[4,128,256]{2,1,0:T(8,128)(2,1)S(1)}, bf16[4,128,256]{2,1,0:T(8,128)(2,1)S(1)}, u32[]{:S(2)}, u32[]{:S(2)}) collective-permute-start(bf16[4,128,256]{2,1,0:T(8,128)(2,1)S(1)} %get-tuple-element.20), channel_id=1, source_target_pairs={{0,1},{1,0},{2,3},{3,2},{4,5},{5,4},{6,7},{7,6},{8,9},{9,8},{10,11... | collective-permute-start | bytes 786440 | tf_op jit(solution)/shard_map/ppermute | solution.py:269
  47.2 2.1 %collective-permute-start.12 = (bf16[4,128,256]{2,1,0:T(8,128)(2,1)S(1)}, bf16[4,128,256]{2,1,0:T(8,128)(2,1)S(1)}, u32[]{:S(2)}, u32[]{:S(2)}) collective-permute-start(bf16[4,128,256]{2,1,0:T(8,128)(2,1)S(1)} %get-tuple-element.19), channel_id=1, source_target_pairs={{0,1},{1,0},{2,3},{3,2},{4,5},{5,4},{6,7},{7,6},{8,9},{9,8},{10,11... | collective-permute-start | bytes 786440 | tf_op jit(solution)/shard_map/ppermute | solution.py:269
